TPU v7x, 128 devices: a whole 4x4x4 slice. The times are simulated.
128 devices in a mesh: dp: 4 (over z), expert: 32 (over y, x, core).
Axes of the slice: x: 4, y: 4, z: 4, core: 2. Of those that a mesh axis runs over, the one named last changes fastest.
Arguments:
- tokens: bfloat16 [4096, 4096], P('expert'), may hold values from -6 to 6
- expert_ids: int32 [4096, 8], P('expert'), may hold values from 0 to 63, all different within a row; in each aligned block of 128 rows (0 to 127, 128 to 255, ...) at most 32 rows name the same one
- gate_prob: float32 [4096, 8], P('expert'), may hold values from 0.02 to 0.3
- gate_weight: bfloat16 [64, 4096, 1536], P('expert', None, 'dp'), may hold values from -0.09375 to 0.09375
- up_weight: bfloat16 [64, 4096, 1536], P('expert', None, 'dp'), may hold values from -0.09375 to 0.09375
- tangent: bfloat16 [64, 1536, 4096], P('expert', None, 'dp'), may hold values from -0.15625 to 0.15625
- curvature: float32 [4096], P('dp'), may hold values from 0.1 to 1.9
Outputs:
- hessian_product: bfloat16 [64, 1536, 4096], P('expert', None, 'dp')
- tangent_image: bfloat16 [4096, 4096], P('expert', 'dp')
Inputs may be any that keep to these rules, and one draw needn't show every extreme that they name: `expert_ids`: each token names 8 different experts. Within each aligned block of 128 tokens no expert is named more than 32 times, and in every draw some expert is named exactly 32 times in some block.
All inputs are finite; a program needn't handle non-finite values.
Results may differ from a plain program's by a relative error of at most 0.007.
Values may be sent and summed in bfloat16 or wider, within the bound.
No kernel may reach another device: no remote copies, remote signals or barrier semaphores. Data moves between devices by JAX's collectives and lax.ppermute only.
A program may use at most 128 MiB of HBM per device.

v0:
```python
import jax
import jax.numpy as jnp
from jax import lax
from jax.sharding import PartitionSpec as P


def slot_of_rows(flat_ids, expert_total, capacity):
    onehot = (flat_ids[:, None] == jnp.arange(expert_total, dtype=jnp.int32)[None, :]).astype(
        jnp.int32
    )
    earlier = jnp.cumsum(onehot, axis=0, dtype=jnp.int32) - onehot
    position = jnp.sum(earlier * onehot, axis=1, dtype=jnp.int32)
    return flat_ids * capacity + position


def row_of_slots(slots, expert_total, capacity):
    row_total = slots.shape[0]
    empty_rows = jnp.full((expert_total * capacity,), row_total, jnp.int32)
    return empty_rows.at[slots].set(jnp.arange(row_total, dtype=jnp.int32))


def per_device(tokens, expert_ids, gate_prob, gate_weight, up_weight, tangent, curvature):
    token_count, width = tokens.shape
    top_count = expert_ids.shape[1]
    local_experts = gate_weight.shape[0]
    groups = lax.axis_size("expert")
    expert_total = local_experts * groups
    capacity = 2 * token_count * top_count // expert_total
    row_count = token_count * top_count
    quarter = tangent.shape[2]
    slots = slot_of_rows(expert_ids.reshape(row_count), expert_total, capacity)
    owners = row_of_slots(slots, expert_total, capacity)
    owner_tokens = owners // top_count
    shape_out = (groups, local_experts, capacity)
    padded = jnp.concatenate([tokens, jnp.zeros((1, width), tokens.dtype)], axis=0)
    outgoing = padded[owner_tokens].reshape(shape_out + (width,))
    arrived = lax.all_to_all(outgoing, "expert", split_axis=0, concat_axis=0, tiled=True)
    gate_pre = jnp.einsum(
        "sxcd,xdf->xscf", arrived, gate_weight, preferred_element_type=jnp.float32
    )
    up_pre = jnp.einsum("sxcd,xdf->xscf", arrived, up_weight, preferred_element_type=jnp.float32)
    hidden_share = (jax.nn.silu(gate_pre) * up_pre).astype(jnp.bfloat16)
    hidden = lax.all_gather(hidden_share, "dp", axis=3, tiled=True)
    expert_out = jnp.einsum(
        "xscf,xfd->sxcd", hidden, tangent, preferred_element_type=jnp.float32
    ).astype(jnp.bfloat16)
    returned = lax.all_to_all(expert_out, "expert", split_axis=0, concat_axis=0, tiled=True)
    per_row = returned.reshape(expert_total * capacity, quarter)[slots].reshape(
        token_count, top_count, quarter
    )
    combined = jnp.sum(gate_prob[:, :, None] * per_row.astype(jnp.float32), axis=1)
    tangent_image = combined.astype(jnp.bfloat16)
    weighted = curvature[None, :] * combined
    scaled = (gate_prob[:, :, None] * weighted[:, None, :]).reshape(row_count, quarter)
    padded_scaled = jnp.concatenate([scaled, jnp.zeros((1, quarter), jnp.float32)], axis=0)
    outgoing_scaled = padded_scaled[owners].astype(jnp.bfloat16).reshape(shape_out + (quarter,))
    incoming = lax.all_to_all(outgoing_scaled, "expert", split_axis=0, concat_axis=0, tiled=True)
    hessian_product = jnp.einsum(
        "xscf,sxcd->xfd", hidden, incoming, preferred_element_type=jnp.float32
    ).astype(jnp.bfloat16)
    return (hessian_product, tangent_image)


def solution(mesh):
    placed = (
        P("expert", None),
        P("expert", None),
        P("expert", None),
        P("expert", None, "dp"),
        P("expert", None, "dp"),
        P("expert", None, "dp"),
        P("dp"),
    )
    return jax.shard_map(
        per_device,
        mesh=mesh,
        in_specs=placed,
        out_specs=(P("expert", None, "dp"), P("expert", "dp")),
        check_vma=False,
    )
```

profile of v0, /device:TPU:1, one launch (start us, length us, event | category | flops | bytes accessed | tf_op | source)
XLA Modules:
  0.0 501.7 jit_solution(15067345853424834301)
XLA Ops:
  7.2 0.8 copy.23
  8.0 0.1 eq.29
  8.1 0.1 eq.25
  8.2 0.7 broadcast_multiply_fusion.1
  8.9 18.0 %reduce-window.6 = s32[64,8,128]{2,1,0:T(8,128)S(1)} reduce-window(s32[64,8,128]{2,1,0:T(8,128)S(1)} %fusion.19, s32[]{:T(128)} %constant.18.clone.1), window={size=1x1x128 pad=0_0x0_0x127_0}, to_apply=%region_0.0 | reduce-window | flops 8323072 | bytes 524292 | tf_op jit(solution)/shard_map/reduce-window
  26.9 0.1 slice.14
  27.0 0.1 copy.25
  27.2 0.1 copy.26
  27.3 0.1 broadcast_add_fusion
  27.5 0.1 copy.22
  27.6 0.1 mul.66
  27.8 4.3 scatter_custom_fusion
  32.1 1.3 concatenate.6
  33.4 14.3 %gather_fusion = bf16[2048,4096]{1,0:T(8,128)(2,1)} fusion(bf16[129,4096]{1,0:T(8,128)(2,1)S(1)} %concatenate.6, s32[2048]{0:T(1024)S(1)} %get-tuple-element.5), kind=kCustom, calls=%fused_computation | custom fusion | bytes 33562624 | tf_op jit(solution)/shard_map/gather | solution.py:36
  47.8 194.3 %all_to_all.15 = bf16[32,2,32,4096]{3,2,1,0:T(8,128)(2,1)S(1)} all-to-all(bf16[32,2,32,4096]{3,2,1,0:T(8,128)(2,1)} %bitcast.54), channel_id=1, replica_groups=mesh['dp'=4,'expert'=32] {'expert'}, dimensions={0} | all-to-all | bytes 33554432 | tf_op jit(solution)/shard_map/all_to_all | solution.py:37
  242.1 12.0 %fusion.2 = f32[2,32,32,384]{3,2,1,0:T(8,128)} fusion(bf16[32,2,32,4096]{3,2,1,0:T(8,128)(2,1)S(1)} %all_to_all.15, bf16[2,4096,384]{2,1,0:T(8,128)(2,1)} %param.10), kind=kOutput, calls=%fused_computation.6 | convolution fusion | flops 6442450944 | bytes 26214400 | tf_op jit(solution)/shard_map/sxcd,xdf->xscf/dot_general | solution.py:38
  254.1 12.4 %multiply_convert_fusion = bf16[2,32,32,384]{3,2,1,0:T(8,128)(2,1)} fusion(f32[2,32,32,384]{3,2,1,0:T(8,128)} %fusion.2, bf16[2,4096,384]{2,1,0:T(8,128)(2,1)} %param.11, bf16[32,2,32,4096]{3,2,1,0:T(8,128)(2,1)S(1)} %all_to_all.15), kind=kOutput, calls=%fused_computation.18 | convolution fusion | flops 6447169536 | bytes 27787264 | tf_op jit(solution)/shard_map/sxcd,xdf->xscf/dot_general | solution.py:41
  266.5 67.6 %all-gather.2.cloned.1.call-done = bf16[2,32,32,1536]{3,2,1,0:T(8,128)(2,1)} async-done(((bf16[2,32,32,384]{3,2,1,0:T(8,128)(2,1)}), bf16[2,32,32,1536]{3,2,1,0:T(8,128)(2,1)}) %all-gather.2.cloned.1.call-update) | async-done | bytes 6291472 | tf_op jit(solution)/shard_map/all_gather | solution.py:43
  334.2 10.6 %convert_bitcast_fusion = bf16[32,2,32,1024]{3,2,0,1:T(8,128)(2,1)S(1)} fusion(bf16[2,32,32,1536]{3,2,1,0:T(8,128)(2,1)} %all-gather.2.cloned.1.call-done, bf16[2,1536,1024]{2,1,0:T(8,128)(2,1)} %param.12), kind=kOutput, calls=%fused_computation.17 | convolution fusion | flops 6444548096 | bytes 16777216 | tf_op jit(solution)/shard_map/xscf,xfd->sxcd/dot_general | solution.py:44
  344.8 2.5 copy.31
  347.2 7.8 %all-to-all-start.1 = ((bf16[32,2,32,1024]{3,2,1,0:T(8,128)(2,1)}), bf16[32,2,32,1024]{3,2,1,0:T(8,128)(2,1)}, u32[]{:S(2)}, u32[]{:S(2)}) async-start(bf16[32,2,32,1024]{3,2,1,0:T(8,128)(2,1)} %copy.31), calls=%async_computation.1 | async-start | bytes 8388608 | tf_op jit(solution)/shard_map/all_to_all | solution.py:47
  355.0 0.1 copy.29
  355.1 0.1 mul.70
  355.2 49.9 %all-to-all-done.1 = bf16[32,2,32,1024]{3,2,1,0:T(8,128)(2,1)} async-done(((bf16[32,2,32,1024]{3,2,1,0:T(8,128)(2,1)}), bf16[32,2,32,1024]{3,2,1,0:T(8,128)(2,1)}, u32[]{:S(2)}, u32[]{:S(2)}) %all-to-all-start.1) | async-done | bytes 4194336 | tf_op jit(solution)/shard_map/all_to_all | solution.py:47
  405.2 7.7 %gather_fusion.1 = bf16[1024,1024]{1,0:T(8,128)(2,1)S(1)} fusion(bf16[2048,1024]{1,0:T(8,128)(2,1)} %bitcast.12, s32[1024]{0:T(1024)S(1)} %broadcast_clamp_fusion), kind=kCustom, calls=%fused_computation.1 | custom fusion | bytes 4198400 | tf_op jit(solution)/shard_map/gather | solution.py:48
  412.9 1.3 fusion.8
  414.2 0.8 fusion.26
  415.0 0.3 bitcast_multiply_fusion
  415.3 0.2 concatenate.7
  415.5 9.6 %gather_fusion.2 = bf16[2048,1024]{1,0:T(8,128)(2,1)} fusion(bf16[1025,1024]{1,0:T(8,128)(2,1)S(1)} %concatenate.7, s32[2048]{0:T(1024)S(1)} %get-tuple-element.4), kind=kCustom, calls=%fused_computation.2 | custom fusion | bytes 8396800 | tf_op jit(solution)/shard_map/gather | solution.py:56
  425.1 58.3 %all_to_all.16 = bf16[32,2,32,1024]{3,2,1,0:T(8,128)(2,1)S(1)} all-to-all(bf16[32,2,32,1024]{3,2,1,0:T(8,128)(2,1)} %bitcast.55), channel_id=1, replica_groups=mesh['dp'=4,'expert'=32] {'expert'}, dimensions={0} | all-to-all | bytes 8388608 | tf_op jit(solution)/shard_map/all_to_all | solution.py:57
  483.4 11.5 %bitcast_convert_fusion = bf16[2,1536,1024]{2,1,0:T(8,128)(2,1)} fusion(bf16[2,32,32,1536]{3,2,1,0:T(8,128)(2,1)} %all-gather.2.cloned.1.call-done, bf16[32,2,32,1024]{3,2,1,0:T(8,128)(2,1)S(1)} %all_to_all.16), kind=kOutput, calls=%fused_computation.8 | convolution fusion | flops 6445596672 | bytes 16777216 | tf_op jit(solution)/shard_map/xscf,sxcd->xfd/dot_general | solution.py:58
  (14 shorter events, 0.2 us)
Async XLA Ops:
  7.2 327.0 %all-gather.2.cloned.1.call-start = ((), (), s32[]{:S(2)}) async-start(), calls=%async_computation.3 | async-start | bytes 7864320 | tf_op jit(solution)/shard_map/all_gather | solution.py:43
  347.2 7.8 %copy-start.1 = (f32[128,8]{0,1:T(8,128)S(1)}, f32[128,8]{0,1:T(8,128)}, u32[]{:S(2)}) copy-start(f32[128,8]{0,1:T(8,128)} %param.9) | copy-start | bytes 12292
  347.2 57.9 %all-to-all-start.1 = ((bf16[32,2,32,1024]{3,2,1,0:T(8,128)(2,1)}), bf16[32,2,32,1024]{3,2,1,0:T(8,128)(2,1)}, u32[]{:S(2)}, u32[]{:S(2)}) async-start(bf16[32,2,32,1024]{3,2,1,0:T(8,128)(2,1)} %copy.31), calls=%async_computation.1 | async-start | bytes 8388608 | tf_op jit(solution)/shard_map/all_to_all | solution.py:47
  405.2 9.0 %copy-start = (f32[1024]{0:T(1024)S(1)}, f32[1024]{0:T(1024)}, u32[]{:S(2)}) copy-start(f32[1024]{0:T(1024)} %param.13) | copy-start | bytes 12292
Sparse Core Ops, SparseCore 0:
  266.7 67.4 all-gather.1
where the time goes:
time: 502 us
  blocking collectives  253 us (50%)
  waiting for transfers between devices  118 us (24%)
  matrix products  46.6 us (9%)
  local copies, waits for them, and re-layouts  41.6 us (8%)
  other arithmetic  21.3 us (4%)
  between operations  14.2 us (3%)
  starting transfers between devices  7.81 us (2%)
    all_to_all x1, blocking collectives, per_device(): lax.all_to_all(outgoing, 'expert', split_axis=0, concat_axis=0, tiled=True)  194 us
    all_gather x1, waiting for transfers between devices, per_device(): hidden = lax.all_gather(hidden_share, 'dp', axis=3, tiled=True)  67.6 us
    all_to_all x1, blocking collectives, per_device(): lax.all_to_all(outgoing_scaled, 'expert', split_axis=0, concat_axis=0, ti...  58.3 us
    all_to_all x1, waiting for transfers between devices, per_device(): lax.all_to_all(expert_out, 'expert', split_axis=0, concat_axis=0, tiled=T...  49.9 us
    another operation x3, other arithmetic  18.2 us
    gather x1, local copies, waits for them, and re-layouts, per_device(): outgoing = padded[owner_tokens].reshape(shape_out + (width,))  14.3 us
    dot_general x1, matrix products, per_device(): jnp.einsum('sxcd,xdf->xscf', arrived, up_weight, preferred_element_type=j...  12.4 us
    dot_general x1, matrix products, per_device(): jnp.einsum('sxcd,xdf->xscf', arrived, gate_weight, preferred_element_type...  12 us
  transfers between devices with their start and end apart: 2, of which 2 were waited for; matrix products, arithmetic and copies ran while one was open for 0% of the time, Pallas kernels for 0%

commit v1 on v0

--- a/solution.py
+++ b/solution.py
@@ -40,7 +40,14 @@
     )
     up_pre = jnp.einsum("sxcd,xdf->xscf", arrived, up_weight, preferred_element_type=jnp.float32)
     hidden_share = (jax.nn.silu(gate_pre) * up_pre).astype(jnp.bfloat16)
-    hidden = lax.all_gather(hidden_share, "dp", axis=3, tiled=True)
+    ways, here, step = (lax.axis_size("dp"), lax.axis_index("dp"), hidden_share.shape[3])
+    line, have = (hidden_share, 1)
+    while have < ways:
+        line = jnp.concatenate(
+            [line, lax.ppermute(line, "dp", [(d, (d - have) % ways) for d in range(ways)])], axis=3
+        )
+        have = 2 * have
+    hidden = jnp.roll(line, here * step, axis=3)
     expert_out = jnp.einsum(
         "xscf,xfd->sxcd", hidden, tangent, preferred_element_type=jnp.float32
     ).astype(jnp.bfloat16)

time: 502 us -> 553 us (1.10)
  waiting for transfers between devices: 118 us -> 150 us
  local copies, waits for them, and re-layouts: 41.6 us -> 59.7 us
  between operations: 14.2 us -> 0.8 us
  starting transfers between devices: 7.81 us -> 14.3 us
    ppermute x0 -> x2, waiting for transfers between devices: none -> 99.9 us  [per_device(): lax.ppermute(line, 'dp', [(d, (d - have) % ways) for d in range(ways)])]
    all_gather x1 -> x0, waiting for transfers between devices: 67.6 us -> none  [per_device(): hidden = lax.all_gather(hidden_share, 'dp', axis=3, tiled=True)]
    unnamed x6 -> x16, local copies, waits for them, and re-layouts: 0.9 us -> 15.1 us
    ppermute x0 -> x2, starting transfers between devices: none -> 5.8 us  [per_device(): lax.ppermute(line, 'dp', [(d, (d - have) % ways) for d in range(ways)])]
  transfers between devices with their start and end apart: 2 -> 3, of which waited for: 2 -> 3; matrix products, arithmetic and copies ran while one was open for 0% -> 0% of each run, Pallas kernels for 0% -> 0%
where the time goes in v1:
time: 553 us
  blocking collectives  253 us (46%)
  waiting for transfers between devices  150 us (27%)
  local copies, waits for them, and re-layouts  59.7 us (11%)
  matrix products  51.9 us (9%)
  other arithmetic  23.5 us (4%)
  starting transfers between devices  14.3 us (3%)
    all_to_all x1, blocking collectives, per_device(): lax.all_to_all(outgoing, 'expert', split_axis=0, concat_axis=0, tiled=True)  194 us
    ppermute x2, waiting for transfers between devices, per_device(): lax.ppermute(line, 'dp', [(d, (d - have) % ways) for d in range(ways)])  99.9 us
    all_to_all x1, blocking collectives, per_device(): lax.all_to_all(outgoing_scaled, 'expert', split_axis=0, concat_axis=0, ti...  58.2 us
    all_to_all x1, waiting for transfers between devices, per_device(): lax.all_to_all(expert_out, 'expert', split_axis=0, concat_axis=0, tiled=T...  50 us
    another operation x3, other arithmetic  18.2 us
    dot_general x1, matrix products, per_device(): jnp.einsum('sxcd,xdf->xscf', arrived, up_weight, preferred_element_type=j...  15.7 us
    dot_general x1, matrix products, per_device(): jnp.einsum('xscf,sxcd->xfd', hidden, incoming, preferred_element_type=jnp...  15.2 us
    unnamed x16, local copies, waits for them, and re-layouts  15.1 us
  transfers between devices with their start and end apart: 3, of which 3 were waited for; matrix products, arithmetic and copies ran while one was open for 0% of the time, Pallas kernels for 0%

profile of v1, /device:TPU:1, one launch (start us, length us, event | category | flops | bytes accessed | tf_op | source)
XLA Modules:
  0.0 552.6 jit_solution(9747372162353329240)
XLA Ops:
  0.6 0.8 copy.23
  1.6 0.7 broadcast_multiply_fusion.1
  2.3 18.0 %reduce-window.6 = s32[64,8,128]{2,1,0:T(8,128)S(1)} reduce-window(s32[64,8,128]{2,1,0:T(8,128)S(1)} %fusion.23, s32[]{:T(128)} %constant.52.clone.1), window={size=1x1x128 pad=0_0x0_0x127_0}, to_apply=%region_0.0 | reduce-window | flops 8323072 | bytes 524292 | tf_op jit(solution)/shard_map/reduce-window
  21.2 4.3 scatter_custom_fusion
  25.5 1.3 concatenate.16
  26.9 14.3 %gather_fusion = bf16[2048,4096]{1,0:T(8,128)(2,1)} fusion(bf16[129,4096]{1,0:T(8,128)(2,1)S(1)} %concatenate.16, s32[2048]{0:T(1024)S(1)} %get-tuple-element.5), kind=kCustom, calls=%fused_computation | custom fusion | bytes 33562624 | tf_op jit(solution)/shard_map/gather | solution.py:36
  41.1 194.3 %all_to_all.15 = bf16[32,2,32,4096]{3,2,1,0:T(8,128)(2,1)S(1)} all-to-all(bf16[32,2,32,4096]{3,2,1,0:T(8,128)(2,1)} %bitcast.54), channel_id=1, replica_groups=mesh['dp'=4,'expert'=32] {'expert'}, dimensions={0} | all-to-all | bytes 33554432 | tf_op jit(solution)/shard_map/all_to_all | solution.py:37
  235.4 5.7 %copy-done = bf16[32,2,32,4096]{3,2,1,0:T(8,128)(2,1)} copy-done((bf16[32,2,32,4096]{3,2,1,0:T(8,128)(2,1)}, bf16[32,2,32,4096]{3,2,1,0:T(8,128)(2,1)S(1)}, u32[]{:S(2)}) %copy-start) | copy-done | bytes 16777240
  241.2 12.0 %fusion.2 = f32[2,32,32,384]{3,2,1,0:T(8,128)} fusion(bf16[32,2,32,4096]{3,2,1,0:T(8,128)(2,1)S(1)} %all_to_all.15, bf16[2,4096,384]{2,1,0:T(8,128)(2,1)} %param.10), kind=kOutput, calls=%fused_computation.6 | convolution fusion | flops 6442450944 | bytes 26214400 | tf_op jit(solution)/shard_map/sxcd,xdf->xscf/dot_general | solution.py:38
  253.2 15.7 %constant_dynamic-update-slice_fusion.5 = (bf16[2,32,32,3072]{3,2,1,0:T(8,128)(2,1)}, bf16[2,32,32,384]{3,2,1,0:T(8,128)(2,1)S(1)}) fusion(bf16[2,4096,384]{2,1,0:T(8,128)(2,1)} %param.11, bf16[32,2,32,4096]{3,2,1,0:T(8,128)(2,1)} %copy-done, f32[2,32,32,384]{3,2,1,0:T(8,128)} %fusion.2), kind=kOutput, calls=%fused_computation.38 | convolution fusion | flops 6447169536 | bytes 29360128 | tf_op jit(solution)/shard_map/sxcd,xdf->xscf/dot_general | solution.py:41
  268.9 3.8 collective-permute-start
  272.6 33.4 %collective-permute-done = bf16[2,32,32,384]{3,2,1,0:T(8,128)(2,1)S(1)} collective-permute-done((bf16[2,32,32,384]{3,2,1,0:T(8,128)(2,1)S(1)}, bf16[2,32,32,384]{3,2,1,0:T(8,128)(2,1)S(1)}, u32[]{:S(2)}, u32[]{:S(2)}) %collective-permute-start) | collective-permute-done | bytes 1572896 | tf_op jit(solution)/shard_map/ppermute | solution.py:47
  306.0 2.1 pad_maximum_fusion
  308.1 2.0 collective-permute-start.1
  310.2 1.6 constant_dynamic-update-slice_fusion.4
  311.8 66.5 %collective-permute-done.1 = bf16[2,32,32,768]{3,2,1,0:T(8,128)(2,1)} collective-permute-done((bf16[2,32,32,768]{3,2,1,0:T(8,128)(2,1)}, bf16[2,32,32,768]{3,2,1,0:T(8,128)(2,1)}, u32[]{:S(2)}, u32[]{:S(2)}) %collective-permute-start.1) | collective-permute-done | bytes 3145760 | tf_op jit(solution)/shard_map/ppermute | solution.py:47
  378.3 4.0 constant_dynamic-update-slice_fusion.3
  382.3 1.4 constant_dynamic-update-slice_fusion.2
  383.8 1.4 constant_dynamic-update-slice_fusion.1
  385.2 3.9 constant_dynamic-update-slice_fusion
  389.1 8.9 %convert_bitcast_fusion = bf16[32,2,32,1024]{3,2,0,1:T(8,128)(2,1)S(1)} fusion(bf16[2,1536,1024]{2,1,0:T(8,128)(2,1)S(1)} %bitcast.62, bf16[2,32,32,3072]{3,2,1,0:T(8,128)(2,1)} %constant_dynamic-update-slice_fusion, s32[]{:T(128)S(6)} %select_n.39), kind=kOutput, calls=%fused_computation.19 | convolution fusion | flops 6444548096 | bytes 16777220 | tf_op jit(solution)/shard_map/xscf,xfd->sxcd/dot_general | solution.py:51
  398.1 2.5 copy.31
  400.5 8.5 %all-to-all-start.1 = ((bf16[32,2,32,1024]{3,2,1,0:T(8,128)(2,1)}), bf16[32,2,32,1024]{3,2,1,0:T(8,128)(2,1)}, u32[]{:S(2)}, u32[]{:S(2)}) async-start(bf16[32,2,32,1024]{3,2,1,0:T(8,128)(2,1)} %copy.31), calls=%async_computation.1 | async-start | bytes 8388608 | tf_op jit(solution)/shard_map/all_to_all | solution.py:54
  409.2 50.0 %all-to-all-done.1 = bf16[32,2,32,1024]{3,2,1,0:T(8,128)(2,1)} async-done(((bf16[32,2,32,1024]{3,2,1,0:T(8,128)(2,1)}), bf16[32,2,32,1024]{3,2,1,0:T(8,128)(2,1)}, u32[]{:S(2)}, u32[]{:S(2)}) %all-to-all-start.1) | async-done | bytes 4194336 | tf_op jit(solution)/shard_map/all_to_all | solution.py:54
  459.3 7.7 %gather_fusion.1 = bf16[1024,1024]{1,0:T(8,128)(2,1)S(1)} fusion(bf16[2048,1024]{1,0:T(8,128)(2,1)} %bitcast.12, s32[1024]{0:T(1024)S(1)} %broadcast_clamp_fusion), kind=kCustom, calls=%fused_computation.1 | custom fusion | bytes 4198400 | tf_op jit(solution)/shard_map/gather | solution.py:55
  467.0 1.3 fusion.10
  468.3 0.8 fusion.32
  469.1 0.3 bitcast_multiply_fusion
  469.4 0.2 concatenate.19
  469.6 9.6 %gather_fusion.2 = bf16[2048,1024]{1,0:T(8,128)(2,1)} fusion(bf16[1025,1024]{1,0:T(8,128)(2,1)S(1)} %concatenate.19, s32[2048]{0:T(1024)S(1)} %get-tuple-element.4), kind=kCustom, calls=%fused_computation.2 | custom fusion | bytes 8396800 | tf_op jit(solution)/shard_map/gather | solution.py:63
  479.2 58.2 %all_to_all.16 = bf16[32,2,32,1024]{3,2,1,0:T(8,128)(2,1)S(1)} all-to-all(bf16[32,2,32,1024]{3,2,1,0:T(8,128)(2,1)} %bitcast.55), channel_id=1, replica_groups=mesh['dp'=4,'expert'=32] {'expert'}, dimensions={0} | all-to-all | bytes 8388608 | tf_op jit(solution)/shard_map/all_to_all | solution.py:64
  537.4 15.2 %bitcast_convert_fusion = bf16[2,1536,1024]{2,1,0:T(8,128)(2,1)} fusion(bf16[2,32,32,3072]{3,2,1,0:T(8,128)(2,1)} %constant_dynamic-update-slice_fusion, s32[]{:T(128)S(6)} %select_n.39, bf16[32,2,32,1024]{3,2,1,0:T(8,128)(2,1)S(1)} %all_to_all.16), kind=kOutput, calls=%fused_computation.8 | convolution fusion | flops 6445596672 | bytes 16777220 | tf_op jit(solution)/shard_map/xscf,sxcd->xfd/dot_general | solution.py:65
  (28 shorter events, 1.2 us)
Async XLA Ops:
  235.4 5.7 %copy-start = (bf16[32,2,32,4096]{3,2,1,0:T(8,128)(2,1)}, bf16[32,2,32,4096]{3,2,1,0:T(8,128)(2,1)S(1)}, u32[]{:S(2)}) copy-start(bf16[32,2,32,4096]{3,2,1,0:T(8,128)(2,1)S(1)} %all_to_all.15) | copy-start | bytes 50331652
  268.9 37.1 %collective-permute-start = (bf16[2,32,32,384]{3,2,1,0:T(8,128)(2,1)S(1)}, bf16[2,32,32,384]{3,2,1,0:T(8,128)(2,1)S(1)}, u32[]{:S(2)}, u32[]{:S(2)}) collective-permute-start(bf16[2,32,32,384]{3,2,1,0:T(8,128)(2,1)S(1)} %get-tuple-element.7), channel_id=1, source_target_pairs={{0,96},{32,0},{64,32},{96,64},{1,97},{33,1},{65,33},{97,65},{2,98}... | collective-permute-start | bytes 4718600 | tf_op jit(solution)/shard_map/ppermute | solution.py:47
  308.1 70.2 %collective-permute-start.1 = (bf16[2,32,32,768]{3,2,1,0:T(8,128)(2,1)}, bf16[2,32,32,768]{3,2,1,0:T(8,128)(2,1)}, u32[]{:S(2)}, u32[]{:S(2)}) collective-permute-start(bf16[2,32,32,768]{3,2,1,0:T(8,128)(2,1)} %pad_maximum_fusion), channel_id=1, source_target_pairs={{0,64},{32,96},{64,0},{96,32},{1,65},{33,97},{65,1},{97,33},{2,66}... | collective-permute-start | bytes 9437192 | tf_op jit(solution)/shard_map/ppermute | solution.py:47
  378.3 10.8 %slice-start = ((s8[6291456]{0:T(1024)(128)(4,1)}), s8[4194304]{0:T(1024)(128)(4,1)S(1)}, s32[]{:S(2)}) async-start(s8[6291456]{0:T(1024)(128)(4,1)} %bitcast.61), calls=%async_computation.3 | async-start | bytes 8388608
  383.8 5.3 slice-start.1
  400.5 8.5 %copy-start.2 = (f32[128,8]{0,1:T(8,128)S(1)}, f32[128,8]{0,1:T(8,128)}, u32[]{:S(2)}) copy-start(f32[128,8]{0,1:T(8,128)} %param.9) | copy-start | bytes 12292
  400.5 58.8 %all-to-all-start.1 = ((bf16[32,2,32,1024]{3,2,1,0:T(8,128)(2,1)}), bf16[32,2,32,1024]{3,2,1,0:T(8,128)(2,1)}, u32[]{:S(2)}, u32[]{:S(2)}) async-start(bf16[32,2,32,1024]{3,2,1,0:T(8,128)(2,1)} %copy.31), calls=%async_computation.1 | async-start | bytes 8388608 | tf_op jit(solution)/shard_map/all_to_all | solution.py:54
  459.3 9.0 %copy-start.1 = (f32[1024]{0:T(1024)S(1)}, f32[1024]{0:T(1024)}, u32[]{:S(2)}) copy-start(f32[1024]{0:T(1024)} %param.13) | copy-start | bytes 12292
